TPU v7x, 256 devices: a whole 4x4x8 slice. The times are simulated.
256 devices in a mesh: src: 32 (over x, z), tgt: 8 (over y, core).
Axes of the slice: x: 4, y: 4, z: 8, core: 2. Of those that a mesh axis runs over, the one named last changes fastest.
Arguments:
- src_points: float32 [16384, 32], P(('src', 'tgt')), may hold values from -4.5 to 4.5
- log_a: float32 [16384], P(('src', 'tgt')), may hold values from -1 to 1
- tgt_points: float32 [65536, 32], P(('src', 'tgt')), may hold values from -1.5 to 1.5
- log_b: float32 [65536], P(('src', 'tgt')), may hold values from -1 to 1
- g_init: float32 [65536], P(('src', 'tgt')), may hold values from -60 to 1.5
Outputs:
- f_pot: float32 [16384], P(('src', 'tgt'))
- g_pot: float32 [65536], P(('src', 'tgt'))
All inputs are finite; a program needn't handle non-finite values.
Results may differ from a plain program's by a relative error of at most 0.0003.
Values sent between devices are 32-bit elements; how exact they have to be, the bound alone decides.
No kernel may reach another device: no remote copies, remote signals or barrier semaphores. Data moves between devices by JAX's collectives and lax.ppermute only.
A program may use at most 64 MiB of HBM per device.

v0:
```python
import jax
import jax.numpy as jnp
from jax import lax
from jax.sharding import PartitionSpec as P

ITERS = 2


EPSILON = 0.5


def joined(part, axis, combine):
    gathered = jax.tree.map(lambda a: lax.all_gather(a, axis), part)

    def take(source):
        return jax.tree.map(lambda a: lax.dynamic_index_in_dim(a, source, 0, False), gathered)

    return lax.fori_loop(
        1, lax.axis_size(axis), lambda source, state: combine(state, take(source)), take(0)
    )


def combine(first, second):
    newtop = jnp.maximum(first[0], second[0])
    return (newtop, first[1] * jnp.exp(first[0] - newtop) + second[1] * jnp.exp(second[0] - newtop))


def local(src_points, log_a, tgt_points, log_b, g_init):
    sources, weights_a = (
        lax.all_gather(src_points, "tgt", axis=0, tiled=True),
        lax.all_gather(log_a, "tgt", axis=0, tiled=True),
    )
    targets, weights_b, g_now = (
        lax.all_gather(tgt_points, "src", axis=0, tiled=True),
        lax.all_gather(log_b, "src", axis=0, tiled=True),
        lax.all_gather(g_init, "src", axis=0, tiled=True),
    )
    source_sq = jnp.sum(sources * sources, axis=1)
    target_sq = jnp.sum(targets * targets, axis=1)
    cross = lax.dot_general(
        sources,
        targets,
        (((1,), (1,)), ((), ())),
        precision=lax.Precision.HIGHEST,
        preferred_element_type=jnp.float32,
    )
    distance = source_sq[:, None] + target_sq[None, :] - 2.0 * cross
    src_index = lax.axis_index("src")
    tgt_index = lax.axis_index("tgt")
    share = targets.shape[0] // lax.axis_size("src")
    own_rows = sources.shape[0] // lax.axis_size("tgt")
    f_now = jnp.zeros((sources.shape[0],), jnp.float32)
    g_own = lax.dynamic_slice_in_dim(g_now, src_index * share, share)
    for sweep in range(ITERS):
        terms = weights_b[None, :] + (g_now[None, :] - distance) / EPSILON
        local_top = jnp.max(terms, axis=1)
        row_top = lax.pmax(local_top, "tgt")
        row_sum = lax.psum(jnp.sum(jnp.exp(terms - row_top[:, None]), axis=1), "tgt")
        f_now = -EPSILON * (row_top + jnp.log(row_sum))
        column_terms = weights_a[:, None] + (f_now[:, None] - distance) / EPSILON
        column_local = jnp.max(column_terms, axis=0)
        column_sum_local = jnp.sum(jnp.exp(column_terms - column_local[None, :]), axis=0)
        column_top, column_sum = joined((column_local, column_sum_local), "src", combine)
        g_now = -EPSILON * (column_top + jnp.log(column_sum))
        g_own = lax.dynamic_slice_in_dim(g_now, src_index * share, share)
    f_own = lax.dynamic_slice_in_dim(f_now, tgt_index * own_rows, own_rows)
    return (f_own, g_own)


def solution(mesh):
    placed = (
        P(("src", "tgt"), None),
        P(("src", "tgt")),
        P(("src", "tgt"), None),
        P(("src", "tgt")),
        P(("src", "tgt")),
    )
    return jax.shard_map(
        local,
        mesh=mesh,
        in_specs=placed,
        out_specs=(P(("src", "tgt")), P(("src", "tgt"))),
        check_vma=False,
    )
```

profile of v0, /device:TPU:1, one launch (start us, length us, event | category | flops | bytes accessed | tf_op | source)
XLA Modules:
  0.0 553.7 jit_solution(5637706899258592222)
XLA Ops:
  7.2 0.7 all-gather.13.cloned.1.call-update
  8.0 16.0 %all-gather.6 = f32[8,64,32]{1,2,0:T(8,128)S(1)} all-gather(f32[1,64,32]{1,2,0:T(8,128)} %bitcast.32), channel_id=1, replica_groups=mesh['src'=32,'tgt'=8] {'tgt'}, dimensions={0}, use_global_device_ids=true | all-gather | bytes 73728 | tf_op jit(solution)/shard_map/all_gather | solution.py:30
  24.0 0.1 copy.8
  24.1 0.1 reshape.36
  24.2 1.3 dynamic-slice
  26.1 0.9 dynamic-update-slice
  27.0 35.9 %all-gather.4 = f32[32,1,256]{2,1,0:T(1,128)S(1)} all-gather(f32[1,1,256]{2,1,0:T(1,128)} %bitcast.33), channel_id=1, replica_groups=mesh['src'=32,'tgt'=8] {'src'}, dimensions={0}, use_global_device_ids=true | all-gather | bytes 33792 | tf_op jit(solution)/shard_map/all_gather | solution.py:35
  62.8 33.6 %all-gather.5 = f32[32,1,256]{2,1,0:T(1,128)S(1)} all-gather(f32[1,1,256]{2,1,0:T(1,128)} %bitcast.34), channel_id=1, replica_groups=mesh['src'=32,'tgt'=8] {'src'}, dimensions={0}, use_global_device_ids=true | all-gather | bytes 33792 | tf_op jit(solution)/shard_map/all_gather | solution.py:36
  96.5 1.4 multiply_reduce_fusion
  97.9 20.3 %fusion = (f32[512]{0:T(512)S(1)}, f32[512,8192]{1,0:T(8,128)}) fusion(f32[8192]{0:T(1024)S(1)} %bitcast.30, f32[8192]{0:T(1024)S(1)} %bitcast.26, f32[512,32]{0,1:T(8,128)S(1)} %reshape.36, f32[8192,32]{0,1:T(8,128)} %all-gather.13.cloned.1.call-done, f32[8192]{0:T(1024)S(1)} %multiply_reduce_fusion, f32[512]{0:T(512)S(1)} %multiply_reduce_fusion.1), kind=kOutput, calls=%fused_computation.15 | convolution fusion | flops 1639972352 | bytes 17993728 | tf_op jit(solution)/shard_map/dot_general | solution.py:40
  118.1 29.0 %pmax.14 = f32[512]{0:T(512)S(1)} all-reduce(f32[512]{0:T(512)S(1)} %get-tuple-element.302), channel_id=1, replica_groups=mesh['src'=32,'tgt'=8] {'tgt'}, use_global_device_ids=true, to_apply=%region_3.0 | all-reduce | flops 512 | bytes 4096 | tf_op jit(solution)/shard_map/pmax | solution.py:57
  147.1 8.1 %exponential_reduce_fusion.3 = f32[512]{0:T(512)S(1)} fusion(f32[512,8192]{1,0:T(8,128)} %get-tuple-element.303, f32[512]{0:T(512)S(1)} %pmax.14, f32[8192]{0:T(1024)S(1)} %bitcast.31, f32[8192]{0:T(1024)S(1)} %bitcast.27), kind=kLoop, calls=%fused_computation.12 | loop fusion | flops 20971008 | bytes 16846848 | tf_op jit(solution)/shard_map/reduce_sum | solution.py:58
  155.2 12.4 %all-reduce.1 = (f32[512]{0:T(512)S(1)}, f32[512]{0:T(512)S(1)}) all-reduce(f32[512]{0:T(512)S(1)} %exponential_reduce_fusion.3, f32[512]{0:T(512)S(1)} %dynamic-update-slice), channel_id=1, replica_groups=mesh['src'=32,'tgt'=8] {'tgt'}, use_global_device_ids=true, to_apply=%region_5.0 | all-reduce | flops 1024 | bytes 8192 | tf_op jit(solution)/shard_map/psum | solution.py:58
  167.6 8.9 %fusion.1 = f32[8192]{0:T(1024)S(1)} fusion(f32[512,8192]{1,0:T(8,128)} %get-tuple-element.303, f32[512]{0:T(512)S(1)} %add_multiply_fusion.2, f32[512]{0:T(512)S(1)} %get-tuple-element.293), kind=kLoop, calls=%fused_computation.16 | loop fusion | flops 16769024 | bytes 16814080 | tf_op jit(solution)/shard_map/reduce_max | solution.py:61
  176.6 8.7 %exponential_reduce_fusion.2 = f32[8192]{0:T(1024)} fusion(f32[512,8192]{1,0:T(8,128)} %get-tuple-element.303, f32[8192]{0:T(1024)S(1)} %fusion.1, f32[512]{0:T(512)S(1)} %add_multiply_fusion.2, f32[512]{0:T(512)S(1)} %get-tuple-element.293), kind=kLoop, calls=%fused_computation.10 | loop fusion | flops 20963328 | bytes 16846848 | tf_op jit(solution)/shard_map/reduce_sum | solution.py:62
  185.3 0.7 all-gather.15.cloned.1.call-update
  186.0 0.2 all-gather.21.cloned.1.call-start
  186.2 65.6 %all-gather.17.cloned.1.call-done = f32[262144]{0:T(1024)} async-done(((f32[8192]{0:T(1024)}), f32[262144]{0:T(1024)}) %all-gather.17.cloned.1.call-update) | async-done | bytes 1048592 | tf_op jit(solution)/shard_map/all_gather | solution.py:13
  251.8 1.4 reshape.17
  253.2 0.8 slice.9
  254.0 74.2 %all-gather.15.cloned.1.call-done = f32[262144]{0:T(1024)} async-done(((f32[8192]{0:T(1024)}), f32[262144]{0:T(1024)}) %all-gather.15.cloned.1.call-update) | async-done | bytes 1048592 | tf_op jit(solution)/shard_map/all_gather | solution.py:13
  328.2 1.4 reshape.16
  329.6 0.8 slice.8
  330.4 3.7 while.34
  330.5 0.1 constant_dynamic-slice_fusion.6
  331.1 0.1 constant_dynamic-slice_fusion.6
  331.4 0.1 constant_dynamic-slice_fusion.6
  332.4 0.1 constant_dynamic-slice_fusion.6
  332.8 0.1 constant_dynamic-slice_fusion.6
  333.4 0.1 constant_dynamic-slice_fusion.6
  333.7 0.1 constant_dynamic-slice_fusion.6
  334.1 8.2 %fusion.2 = f32[512]{0:T(512)S(1)} fusion(f32[512,8192]{1,0:T(8,128)} %get-tuple-element.303, f32[8192]{0:T(1024)S(1)} %add_multiply_fusion, f32[8192]{0:T(1024)S(1)} %bitcast.28), kind=kLoop, calls=%fused_computation.17 | loop fusion | flops 16776704 | bytes 16844800 | tf_op jit(solution)/shard_map/reduce_max | solution.py:56
  342.3 16.8 %pmax.15 = f32[512]{0:T(512)S(1)} all-reduce(f32[512]{0:T(512)S(1)} %fusion.2), channel_id=1, replica_groups=mesh['src'=32,'tgt'=8] {'tgt'}, use_global_device_ids=true, to_apply=%region_11.12 | all-reduce | flops 512 | bytes 4096 | tf_op jit(solution)/shard_map/pmax | solution.py:57
  359.1 8.1 %exponential_reduce_fusion.1 = f32[512]{0:T(512)S(1)} fusion(f32[512,8192]{1,0:T(8,128)} %get-tuple-element.303, f32[512]{0:T(512)S(1)} %pmax.15, f32[8192]{0:T(1024)S(1)} %add_multiply_fusion, f32[8192]{0:T(1024)S(1)} %bitcast.29), kind=kLoop, calls=%fused_computation.8 | loop fusion | flops 20971008 | bytes 16846848 | tf_op jit(solution)/shard_map/reduce_sum | solution.py:58
  367.1 12.4 %psum.15 = f32[512]{0:T(512)S(1)} all-reduce(f32[512]{0:T(512)S(1)} %exponential_reduce_fusion.1), channel_id=1, replica_groups=mesh['src'=32,'tgt'=8] {'tgt'}, use_global_device_ids=true, to_apply=%region_13.14 | all-reduce | flops 512 | bytes 4096 | tf_op jit(solution)/shard_map/psum | solution.py:58
  379.6 8.9 %fusion.3 = f32[8192]{0:T(1024)S(1)} fusion(f32[512,8192]{1,0:T(8,128)} %get-tuple-element.303, f32[512]{0:T(512)S(1)} %add_multiply_fusion.1, f32[512]{0:T(512)S(1)} %get-tuple-element.293), kind=kLoop, calls=%fused_computation.18 | loop fusion | flops 16769024 | bytes 16814080 | tf_op jit(solution)/shard_map/reduce_max | solution.py:61
  388.5 8.7 %exponential_reduce_fusion = f32[8192]{0:T(1024)} fusion(f32[512,8192]{1,0:T(8,128)} %get-tuple-element.303, f32[8192]{0:T(1024)S(1)} %fusion.3, f32[512]{0:T(512)S(1)} %add_multiply_fusion.1, f32[512]{0:T(512)S(1)} %get-tuple-element.293), kind=kLoop, calls=%fused_computation.6 | loop fusion | flops 20963328 | bytes 16846848 | tf_op jit(solution)/shard_map/reduce_sum | solution.py:62
  397.3 0.5 all-gather.19.cloned.1.call-update
  397.8 0.6 dynamic_slice.61
  398.4 65.9 %all-gather.21.cloned.1.call-done = f32[262144]{0:T(1024)} async-done(((f32[8192]{0:T(1024)}), f32[262144]{0:T(1024)}) %all-gather.21.cloned.1.call-update) | async-done | bytes 1048592 | tf_op jit(solution)/shard_map/all_gather | solution.py:13
  464.3 1.4 reshape.19
  465.7 0.8 slice.11
  466.5 74.1 %all-gather.19.cloned.1.call-done = f32[262144]{0:T(1024)} async-done(((f32[8192]{0:T(1024)}), f32[262144]{0:T(1024)}) %all-gather.19.cloned.1.call-update) | async-done | bytes 1048592 | tf_op jit(solution)/shard_map/all_gather | solution.py:13
  540.6 1.4 reshape.18
  542.0 0.8 slice.10
  542.7 3.7 while.35
  543.1 0.1 constant_dynamic-slice_fusion.7
  546.5 0.7 fusion.4
  (132 shorter events, 5.6 us)
Async XLA Ops:
  7.2 89.3 %all-gather.13.cloned.1.call-start = ((), (), s32[]{:S(2)}) async-start(), calls=%async_computation | async-start | bytes 1081344 | tf_op jit(solution)/shard_map/all_gather | solution.py:34
  7.9 243.9 %all-gather.17.cloned.1.call-start = ((), (), s32[]{:S(2)}) async-start(), calls=%async_computation.2 | async-start | bytes 1081344 | tf_op jit(solution)/shard_map/all_gather | solution.py:13
  176.6 8.7 %copy-start.1 = (f32[8192]{0:T(1024)}, f32[8192]{0:T(1024)S(1)}, u32[]{:S(2)}) copy-start(f32[8192]{0:T(1024)S(1)} %fusion.1) | copy-start | bytes 98308
  185.3 142.9 %all-gather.15.cloned.1.call-start = ((), (), s32[]{:S(2)}) async-start(), calls=%async_computation.1 | async-start | bytes 1081344 | tf_op jit(solution)/shard_map/all_gather | solution.py:13
  186.0 278.3 %all-gather.21.cloned.1.call-start = ((), (), s32[]{:S(2)}) async-start(), calls=%async_computation.4 | async-start | bytes 1081344 | tf_op jit(solution)/shard_map/all_gather | solution.py:13
  388.5 8.7 %copy-start = (f32[8192]{0:T(1024)}, f32[8192]{0:T(1024)S(1)}, u32[]{:S(2)}) copy-start(f32[8192]{0:T(1024)S(1)} %fusion.3) | copy-start | bytes 98308
  397.2 143.3 %all-gather.19.cloned.1.call-start = ((), (), s32[]{:S(2)}) async-start(), calls=%async_computation.3 | async-start | bytes 1081344 | tf_op jit(solution)/shard_map/all_gather | solution.py:13
Sparse Core Ops, SparseCore 0:
  10.5 70.7 all-gather.12
  185.4 66.3 all-gather.16
  254.4 73.7 all-gather.14
  397.3 66.9 all-gather.20
  466.7 73.7 all-gather.18
where the time goes:
time: 558 us; the launch traced here: 554 us
  waiting for transfers between devices  282 us (51%)
  blocking collectives  156 us (28%)
  other arithmetic  63.9 us (11%)
  matrix products  20.3 us (4%)
  local copies, waits for them, and re-layouts  14.9 us (3%)
  between operations  14.6 us (3%)
    all_gather x4, waiting for transfers between devices, joined(): gathered = jax.tree.map(lambda a: lax.all_gather(a, axis), part)  280 us
    pmax x2, blocking collectives, local(): row_top = lax.pmax(local_top, 'tgt')  45.8 us
    all_gather x1, blocking collectives, local(): lax.all_gather(log_b, 'src', axis=0, tiled=True)  35.9 us
    all_gather x1, blocking collectives, local(): lax.all_gather(g_init, 'src', axis=0, tiled=True)  33.6 us
    psum x2, blocking collectives, local(): lax.psum(jnp.sum(jnp.exp(terms - row_top[:, None]), axis=1), 'tgt')  24.8 us
    dot_general x1, matrix products, local(): lax.dot_general(sources, targets, (((1,), (1,)), ((), ())), precision=lax...  20.3 us
    reduce_max x2, other arithmetic, local(): column_local = jnp.max(column_terms, axis=0)  17.9 us
    reduce_sum x2, other arithmetic, local(): jnp.sum(jnp.exp(column_terms - column_local[None, :]), axis=0)  17.3 us
  transfers between devices with their start and end apart: 5, of which 4 were waited for; matrix products, arithmetic and copies ran while one was open for 1% of the time, Pallas kernels for 0%

commit v1 on v0

v1 whole, which is shorter than its diff:
```python
import functools

import jax
import jax.numpy as jnp
import numpy as np
from jax import lax
from jax.experimental import pallas as pl
from jax.experimental.pallas import tpu as pltpu
from jax.sharding import Mesh
from jax.sharding import PartitionSpec as P

EPSILON = 0.5
LOG2E = float(np.log2(np.e))
LN2 = float(np.log(2.0))
AXES = ("x", "z", "y", "c")
SOURCE_AXES = ("z", "c")
TARGET_AXES = ("x", "y")
DIM = 32
DEPTH = 128
VEC = 3 * DIM
TILE = 256
CHUNK = 64
F32 = jnp.float32
BF16 = jnp.bfloat16
PARAMS = pltpu.CompilerParams(vmem_limit_bytes=48 << 20)


def split(v, count):
    pieces = []
    for _ in range(count):
        piece = v.astype(BF16)
        pieces.append(piece.astype(F32))
        v = v - pieces[-1]
    return pieces


def vector_rows(first, second, width):
    def rows(v):
        if v is None:
            return [jnp.ones((1, width), F32)] * 3
        return split(v, 3)

    zeros = jnp.zeros((10, width), F32)
    return jnp.concatenate(rows(first) + rows(second) + [zeros], axis=0).astype(BF16)


def combine(parts):
    top = jnp.max(parts, axis=0)
    return top + jnp.log2(jnp.sum(jnp.exp2(parts - top[None]), axis=0))


def lse_pass(lhs_ref, rhs_ref, write):
    chunks = lhs_ref.shape[0] // CHUNK

    def tile(n, carry):
        rhs = rhs_ref[:, pl.ds(pl.multiple_of(n * TILE, TILE), TILE)]

        def step(r, state):
            top, total = state
            lhs = lhs_ref[pl.ds(pl.multiple_of(r * CHUNK, CHUNK), CHUNK), :]
            terms = jnp.dot(lhs, rhs, preferred_element_type=F32).reshape(CHUNK // 8, 8, TILE)
            newtop = jnp.maximum(top, jnp.max(terms, axis=0))
            added = jnp.sum(jnp.exp2(terms - newtop[None]), axis=0)
            return newtop, total * jnp.exp2(top - newtop) + added

        start = (jnp.full((8, TILE), -1e30, F32), jnp.zeros((8, TILE), F32))
        top, total = lax.fori_loop(0, chunks, step, start, unroll=16)
        peak = jnp.max(top, axis=0, keepdims=True)
        total = jnp.sum(total * jnp.exp2(top - peak), axis=0, keepdims=True)
        write(n, peak + jnp.log2(total))
        return carry

    lax.fori_loop(0, rhs_ref.shape[1] // TILE, tile, 0)


def write_copies(out_ref):
    def write(n, value):
        at = pl.ds(pl.multiple_of(n * TILE, TILE), TILE)
        out_ref[:, :, at] = jnp.broadcast_to(value[None], (out_ref.shape[0], 1, TILE))

    return write


def pack_kernel(src, la, tgt, lb, g, spack, tpack, ssq, tsq):
    s_t = src[...].T
    t_t = tgt[...].T
    s_norm = jnp.sum(s_t * s_t, axis=0, keepdims=True)
    t_norm = jnp.sum(t_t * t_t, axis=0, keepdims=True)
    ssq[...] = s_norm
    tsq[...] = t_norm
    s_t = s_t * ((2.0 / EPSILON) * LOG2E)
    half = DIM // 2
    weights = jnp.concatenate([la[...] * LOG2E, jnp.zeros_like(la[...])], axis=1)
    packed = jnp.concatenate(
        [jnp.concatenate([s_t[:half], s_t[half:]], axis=1), jnp.broadcast_to(weights, (8, weights.shape[1]))], axis=0
    )
    spack[...] = jnp.broadcast_to(packed[None], spack.shape)
    h = (lb[...] + (g[...] - t_norm) / EPSILON) * LOG2E
    rest = jnp.concatenate([h, lb[...] * LOG2E, jnp.zeros((6, h.shape[1]), F32)], axis=0)
    tpack[...] = jnp.broadcast_to(jnp.concatenate([t_t, rest], axis=0)[None], tpack.shape)


def first_kernel(spg, tpg, out, akm, bkm, la, lb, brm, bh):
    groups, _, lanes = spg.shape
    half = DIM // 2
    own = lanes // 2
    pieces = []
    for p in range(0, groups, 2):
        a, b = spg[p], spg[p + 1]
        top = jnp.concatenate([a[:, :own], b[:, :own]], axis=1)
        low = jnp.concatenate([a[:half, own:], b[:half, own:]], axis=1)
        la[:, own * p : own * (p + 2)] = top[half : half + 1]
        pieces.append(jnp.concatenate([top[:half], low], axis=0))
    s = jnp.concatenate(pieces, axis=1)
    s1, s2 = (v.astype(BF16) for v in split(s, 2))
    width = s.shape[1]
    none = jnp.zeros((1, width), F32)
    akm[...] = jnp.concatenate([s1, s1, s2, vector_rows(none, None, width), jnp.zeros((16, width), BF16)], axis=0)
    width = tpg.shape[2]
    none = jnp.zeros((1, width), F32)
    for p in range(tpg.shape[0]):
        at = slice(width * p, width * (p + 1))
        t1, t2 = (v.astype(BF16) for v in split(tpg[p, :DIM], 2))
        h = tpg[p, DIM : DIM + 1]
        lb[:, at] = tpg[p, DIM + 1 : DIM + 2]
        zeros = jnp.zeros((16, width), BF16)
        bkm[:, at] = jnp.concatenate([t1, t2, t1, vector_rows(None, none, width), zeros], axis=0)
        bh[...] = jnp.concatenate([t1, t2, t1, vector_rows(None, h, width), zeros], axis=0)
        brm[at, :] = bh[...].T
    lse_pass(brm, akm, write_copies(out))


def column_kernel(parts, la, akm, bkm, out, arm, tmp):
    k = la[...] - combine(parts[...])
    tmp[...] = akm[...]
    tmp[VEC : VEC + 16, :] = vector_rows(k, None, k.shape[1])
    arm[...] = tmp[...].T
    lse_pass(arm, bkm, write_copies(out))


def row_kernel(parts, lb, akm, bkm, out, brm, tmp):
    h = lb[...] - combine(parts[...])
    tmp[...] = bkm[...]
    tmp[VEC : VEC + 16, :] = vector_rows(None, h, h.shape[1])
    brm[...] = tmp[...].T
    lse_pass(brm, akm, write_copies(out))


def last_column_kernel(parts, la, akm, bkm, ssq, out, f, arm, tmp):
    rows = combine(parts[...])
    me = lax.axis_index(TARGET_AXES)
    own = f.shape[1]
    mine = jnp.zeros((1, own), F32)
    for p in range(rows.shape[1] // own):
        mine = mine + jnp.where(me == p, rows[:, own * p : own * (p + 1)], 0.0)
    f[...] = ssq[...] - (EPSILON * LN2) * mine
    k = la[...] - rows
    tmp[...] = akm[...]
    tmp[VEC : VEC + 16, :] = vector_rows(k, None, k.shape[1])
    arm[...] = tmp[...].T

    def write(n, value):
        out[n] = value

    lse_pass(arm, bkm, write)


def last_kernel(parts, tsq, g):
    g[...] = tsq[...] - (EPSILON * LN2) * combine(parts[...])


def call(kernel, name, outs, *args, scratch=()):
    whole = pl.BlockSpec(memory_space=pltpu.VMEM)
    return pl.pallas_call(
        kernel,
        name=name,
        out_shape=[jax.ShapeDtypeStruct(*o) for o in outs],
        in_specs=[whole] * len(args),
        out_specs=[whole] * len(outs),
        scratch_shapes=list(scratch),
        compiler_params=PARAMS,
    )(*args)


def exchange(v, axes):
    return lax.all_to_all(v, axes, 0, 0, tiled=True)


def local(src_points, log_a, tgt_points, log_b, g_init):
    own_s, own_t = src_points.shape[0], tgt_points.shape[0]
    across_t = lax.axis_size(TARGET_AXES)
    across_s = lax.axis_size(SOURCE_AXES)
    rows, cols = own_s * across_t, own_t * across_s
    row = lambda v: v.reshape(1, -1)
    spack, tpack, ssq, tsq = call(
        pack_kernel,
        "pack",
        [
            ((across_t, DIM // 2 + 8, 2 * own_s), F32),
            ((across_s, DIM + 8, own_t), F32),
            ((1, own_s), F32),
            ((1, own_t), F32),
        ],
        src_points,
        row(log_a),
        tgt_points,
        row(log_b),
        row(g_init),
    )
    spg = exchange(spack, TARGET_AXES)
    tpg = exchange(tpack, SOURCE_AXES)
    row_out = ((across_t, 1, rows), F32)
    col_out = ((across_s, 1, cols), F32)
    parts, akm, bkm, la, lb = call(
        first_kernel,
        "row_pass_first",
        [row_out, ((DEPTH, rows), BF16), ((DEPTH, cols), BF16), ((1, rows), F32), ((1, cols), F32)],
        spg,
        tpg,
        scratch=[pltpu.VMEM((cols, DEPTH), BF16), pltpu.VMEM((DEPTH, own_t), BF16)],
    )
    row_scratch = [pltpu.VMEM((cols, DEPTH), BF16), pltpu.VMEM((DEPTH, cols), BF16)]
    col_scratch = [pltpu.VMEM((rows, DEPTH), BF16), pltpu.VMEM((DEPTH, rows), BF16)]
    parts = exchange(parts, TARGET_AXES)
    (parts,) = call(column_kernel, "column_pass", [col_out], parts, la, akm, bkm, scratch=col_scratch)
    parts = exchange(parts, SOURCE_AXES)
    (parts,) = call(row_kernel, "row_pass", [row_out], parts, lb, akm, bkm, scratch=row_scratch)
    parts = exchange(parts, TARGET_AXES)
    parts, f = call(
        last_column_kernel,
        "column_pass_last",
        [((across_s, 1, own_t), F32), ((1, own_s), F32)],
        parts,
        la,
        akm,
        bkm,
        ssq,
        scratch=col_scratch,
    )
    parts = exchange(parts, SOURCE_AXES)
    (g,) = call(last_kernel, "last", [((1, own_t), F32)], parts, tsq)
    return f.reshape(own_s), g.reshape(own_t)


def solution(mesh):
    fine = Mesh(mesh.devices.reshape(4, 8, 4, 2), AXES)
    flat = P(AXES)
    return jax.shard_map(
        local,
        mesh=fine,
        in_specs=(P(AXES, None), flat, P(AXES, None), flat, flat),
        out_specs=(flat, flat),
        check_vma=False,
    )
```

time: 558 us -> 120 us (0.22)
  waiting for transfers between devices: 282 us -> 0 us
  blocking collectives: 156 us -> 91.3 us
  other arithmetic: 63.9 us -> 0 us
  Pallas kernels: 0 us -> 26.4 us
  matrix products: 20.3 us -> 0 us
  between operations: 14.6 us -> 0.69 us
  local copies, waits for them, and re-layouts: 14.9 us -> 1.58 us
    all_gather x5 -> x0, waiting for transfers between devices: 280 us -> none  [the longest x4 280 us: joined(): gathered = jax.tree.map(lambda a: lax.all_gather(a, axis), part)]
    all_to_all x0 -> x6, blocking collectives: none -> 91.3 us  [exchange(): return lax.all_to_all(v, axes, 0, 0, tiled=True)]
    all_gather x3 -> x0, blocking collectives: 85.5 us -> none  [the longest x1 35.9 us: local(): lax.all_gather(log_b, 'src', axis=0, tiled=True)]
    pmax x2 -> x0, blocking collectives: 45.8 us -> none  [local(): row_top = lax.pmax(local_top, 'tgt')]
    reduce_sum x6 -> x0, other arithmetic: 34.8 us -> none  [the longest x2 17.3 us: local(): jnp.sum(jnp.exp(column_terms - column_local[None, :]), axis=0)]
    pallas_call x0 -> x6, Pallas kernels: none -> 26.4 us  [call(): pl.pallas_call(kernel, name=name, out_shape=[jax.ShapeDtypeStruct(*o) for...]
    reduce_max x3 -> x0, other arithmetic: 26.1 us -> none  [the longest x2 17.9 us: local(): column_local = jnp.max(column_terms, axis=0)]
    psum x2 -> x0, blocking collectives: 24.8 us -> none  [local(): lax.psum(jnp.sum(jnp.exp(terms - row_top[:, None]), axis=1), 'tgt')]
  transfers between devices with their start and end apart: 5 -> 0, of which waited for: 4 -> 0; matrix products, arithmetic and copies ran while one was open for 1% -> 0% of each run, Pallas kernels for 0% -> 0%
where the time goes in v1:
time: 120 us
  blocking collectives  91.3 us (76%)
  Pallas kernels  26.4 us (22%)
  local copies, waits for them, and re-layouts  1.58 us (1%)
    all_to_all x6, blocking collectives, exchange(): return lax.all_to_all(v, axes, 0, 0, tiled=True)  91.3 us
    pallas_call x6, Pallas kernels, call(): pl.pallas_call(kernel, name=name, out_shape=[jax.ShapeDtypeStruct(*o) for...  26.4 us

profile of v1, /device:TPU:1, one launch (start us, length us, event | category | flops | bytes accessed | tf_op | source)
XLA Modules:
  0.0 119.9 jit_solution(12192127817558828822)
XLA Ops:
  0.6 0.0 copy-start.3
  0.6 0.8 copy.7.src
  1.4 0.0 copy-done.3
  1.4 0.1 copy.8.tgt
  1.5 0.0 copy-start.1
  1.6 0.0 copy-start
  1.6 0.0 copy-start.2
  1.6 0.6 copy-done.1
  2.2 0.0 copy-done
  2.2 0.0 copy-done.2
  2.2 0.1 pack.1
  2.4 14.5 %all_to_all.30.spg = f32[16,24,128]{2,1,0:T(8,128)S(1)} all-to-all(f32[16,24,128]{2,1,0:T(8,128)S(1)} %get-tuple-element.13), channel_id=1, replica_groups=mesh['x'=4,'z'=8,'y'=4,'c'=2] {'x','y'}, dimensions={0} | all-to-all | bytes 393216 | tf_op jit(solution)/shard_map/all_to_all | solution.py:186
  16.9 30.5 %all_to_all.31.tpg = f32[16,40,256]{2,1,0:T(8,128)S(1)} all-to-all(f32[16,40,256]{2,1,0:T(8,128)S(1)} %get-tuple-element.14), channel_id=1, replica_groups=mesh['x'=4,'z'=8,'y'=4,'c'=2] {'z','c'}, dimensions={0} | all-to-all | bytes 1310720 | tf_op jit(solution)/shard_map/all_to_all | solution.py:186
  47.4 6.3 %row_pass_first.1 = (f32[16,1,1024]{2,1,0:T(1,128)S(1)}, bf16[128,1024]{1,0:T(8,128)(2,1)S(1)}, bf16[128,4096]{1,0:T(8,128)(2,1)S(1)}, f32[1,1024]{1,0:T(1,128)S(1)}, f32[1,4096]{1,0:T(1,128)S(1)}) custom-call(f32[16,24,128]{2,1,0:T(8,128)S(1)} %all_to_all.30.spg, f32[16,40,256]{2,1,0:T(8,128)S(1)} %all_to_all.31.tpg), custom_call_target="tpu_custom_call" | custom-call | tf_op jit(solution)/shard_map/row_pass_first/pallas_call | solution.py:174
  53.7 9.7 %all_to_all.32.parts = f32[16,1,1024]{2,1,0:T(1,128)S(1)} all-to-all(f32[16,1,1024]{2,1,0:T(1,128)S(1)} %get-tuple-element.15), channel_id=1, replica_groups=mesh['x'=4,'z'=8,'y'=4,'c'=2] {'x','y'}, dimensions={0} | all-to-all | bytes 131072 | tf_op jit(solution)/shard_map/all_to_all | solution.py:186
  63.4 6.4 %column_pass.1 = f32[16,1,4096]{2,1,0:T(1,128)S(1)} custom-call(f32[16,1,1024]{2,1,0:T(1,128)S(1)} %all_to_all.32.parts, f32[1,1024]{1,0:T(1,128)S(1)} %get-tuple-element.16.la, bf16[128,1024]{1,0:T(8,128)(2,1)S(1)} %get-tuple-element.17.akm, bf16[128,4096]{1,0:T(8,128)(2,1)S(1)} %get-tuple-element.18.bkm), custom_call_target="tpu_custom_call" | custom-call | tf_op jit(solution)/shard_map/column_pass/pallas_call | solution.py:174
  69.8 15.7 %all_to_all.33.parts = f32[16,1,4096]{2,1,0:T(1,128)S(1)} all-to-all(f32[16,1,4096]{2,1,0:T(1,128)S(1)} %column_pass.1), channel_id=1, replica_groups=mesh['x'=4,'z'=8,'y'=4,'c'=2] {'z','c'}, dimensions={0} | all-to-all | bytes 524288 | tf_op jit(solution)/shard_map/all_to_all | solution.py:186
  85.5 6.5 %row_pass.1 = f32[16,1,1024]{2,1,0:T(1,128)S(1)} custom-call(f32[16,1,4096]{2,1,0:T(1,128)S(1)} %all_to_all.33.parts, f32[1,4096]{1,0:T(1,128)S(1)} %get-tuple-element.19.lb, bf16[128,1024]{1,0:T(8,128)(2,1)S(1)} %get-tuple-element.17.akm, bf16[128,4096]{1,0:T(8,128)(2,1)S(1)} %get-tuple-element.18.bkm), custom_call_target="tpu_custom_call" | custom-call | tf_op jit(solution)/shard_map/row_pass/pallas_call | solution.py:174
  91.9 9.6 %all_to_all.34.parts = f32[16,1,1024]{2,1,0:T(1,128)S(1)} all-to-all(f32[16,1,1024]{2,1,0:T(1,128)S(1)} %row_pass.1), channel_id=1, replica_groups=mesh['x'=4,'z'=8,'y'=4,'c'=2] {'x','y'}, dimensions={0} | all-to-all | bytes 131072 | tf_op jit(solution)/shard_map/all_to_all | solution.py:186
  101.5 6.5 %column_pass_last.1 = (f32[16,1,256]{2,1,0:T(1,128)S(1)}, f32[1,64]{1,0:T(1,128)}) custom-call(f32[16,1,1024]{2,1,0:T(1,128)S(1)} %all_to_all.34.parts, f32[1,1024]{1,0:T(1,128)S(1)} %get-tuple-element.16.la, bf16[128,1024]{1,0:T(8,128)(2,1)S(1)} %get-tuple-element.17.akm, bf16[128,4096]{1,0:T(8,128)(2,1)S(1)} %get-tuple-element.18.bkm, ...), custom_call_target="tpu_custom_call" | custom-call | tf_op jit(solution)/shard_map/column_pass_last/pallas_call | solution.py:174
  108.0 11.3 %all_to_all.35.parts = f32[16,1,256]{2,1,0:T(1,128)S(1)} all-to-all(f32[16,1,256]{2,1,0:T(1,128)S(1)} %get-tuple-element.22), channel_id=1, replica_groups=mesh['x'=4,'z'=8,'y'=4,'c'=2] {'z','c'}, dimensions={0} | all-to-all | bytes 32768 | tf_op jit(solution)/shard_map/all_to_all | solution.py:186
  119.3 0.6 last.1
Async XLA Ops:
  0.6 0.8 copy-start.3
  1.5 0.7 copy-start.1
  1.6 0.7 copy-start
  1.6 0.7 copy-start.2

commit v2 on v1

--- a/solution.py
+++ b/solution.py
@@ -13,13 +13,13 @@
 LOG2E = float(np.log2(np.e))
 LN2 = float(np.log(2.0))
 AXES = ("x", "z", "y", "c")
-SOURCE_AXES = ("z", "c")
-TARGET_AXES = ("x", "y")
+SOURCE_AXES = ("x", "y")
+TARGET_AXES = ("z", "c")
 DIM = 32
 DEPTH = 128
 VEC = 3 * DIM
-TILE = 256
-CHUNK = 64
+TILE = 512
+CHUNK = 128
 F32 = jnp.float32
 BF16 = jnp.bfloat16
 PARAMS = pltpu.CompilerParams(vmem_limit_bytes=48 << 20)
@@ -50,33 +50,26 @@
 
 
 def lse_pass(lhs_ref, rhs_ref, write):
-    chunks = lhs_ref.shape[0] // CHUNK
-
-    def tile(n, carry):
-        rhs = rhs_ref[:, pl.ds(pl.multiple_of(n * TILE, TILE), TILE)]
-
-        def step(r, state):
-            top, total = state
-            lhs = lhs_ref[pl.ds(pl.multiple_of(r * CHUNK, CHUNK), CHUNK), :]
-            terms = jnp.dot(lhs, rhs, preferred_element_type=F32).reshape(CHUNK // 8, 8, TILE)
-            newtop = jnp.maximum(top, jnp.max(terms, axis=0))
+    for at in range(0, rhs_ref.shape[1], TILE):
+        rhs = rhs_ref[:, at : at + TILE]
+        top = total = None
+        for row in range(0, lhs_ref.shape[0], CHUNK):
+            terms = jnp.dot(lhs_ref[row : row + CHUNK, :], rhs, preferred_element_type=F32)
+            terms = terms.reshape(CHUNK // 8, 8, TILE)
+            newtop = jnp.max(terms, axis=0)
+            if top is not None:
+                newtop = jnp.maximum(top, newtop)
             added = jnp.sum(jnp.exp2(terms - newtop[None]), axis=0)
-            return newtop, total * jnp.exp2(top - newtop) + added
-
-        start = (jnp.full((8, TILE), -1e30, F32), jnp.zeros((8, TILE), F32))
-        top, total = lax.fori_loop(0, chunks, step, start, unroll=16)
+            total = added if top is None else total * jnp.exp2(top - newtop) + added
+            top = newtop
         peak = jnp.max(top, axis=0, keepdims=True)
         total = jnp.sum(total * jnp.exp2(top - peak), axis=0, keepdims=True)
-        write(n, peak + jnp.log2(total))
-        return carry
-
-    lax.fori_loop(0, rhs_ref.shape[1] // TILE, tile, 0)
+        write(at, peak + jnp.log2(total))
 
 
 def write_copies(out_ref):
-    def write(n, value):
-        at = pl.ds(pl.multiple_of(n * TILE, TILE), TILE)
-        out_ref[:, :, at] = jnp.broadcast_to(value[None], (out_ref.shape[0], 1, TILE))
+    def write(at, value):
+        out_ref[:, :, at : at + TILE] = jnp.broadcast_to(value[None], (out_ref.shape[0], 1, TILE))
 
     return write
 
@@ -159,8 +152,9 @@
     tmp[VEC : VEC + 16, :] = vector_rows(k, None, k.shape[1])
     arm[...] = tmp[...].T
 
-    def write(n, value):
-        out[n] = value
+    def write(at, value):
+        for own in range(0, TILE, out.shape[2]):
+            out[(at + own) // out.shape[2]] = value[:, own : own + out.shape[2]]
 
     lse_pass(arm, bkm, write)
 

time: 120 us -> 101 us (0.84)
  Pallas kernels: 26.4 us -> 15.8 us
  blocking collectives: 91.3 us -> 83 us
    pallas_call x6, Pallas kernels: 26.4 us -> 15.8 us  [call(): pl.pallas_call(kernel, name=name, out_shape=[jax.ShapeDtypeStruct(*o) for...]
    all_to_all x6, blocking collectives: 91.3 us -> 83 us  [exchange(): return lax.all_to_all(v, axes, 0, 0, tiled=True)]
where the time goes in v2:
time: 101 us
  blocking collectives  83 us (82%)
  Pallas kernels  15.8 us (16%)
  local copies, waits for them, and re-layouts  1.58 us (2%)
    all_to_all x6, blocking collectives, exchange(): return lax.all_to_all(v, axes, 0, 0, tiled=True)  83 us
    pallas_call x6, Pallas kernels, call(): pl.pallas_call(kernel, name=name, out_shape=[jax.ShapeDtypeStruct(*o) for...  15.8 us

profile of v2, /device:TPU:1, one launch (start us, length us, event | category | flops | bytes accessed | tf_op | source)
XLA Modules:
  0.0 101.1 jit_solution(6675265965475072358)
XLA Ops:
  0.6 0.0 copy-start.3
  0.6 0.8 copy.7.src
  1.4 0.0 copy-done.3
  1.4 0.1 copy.8.tgt
  1.5 0.0 copy-start.1
  1.6 0.0 copy-start
  1.6 0.0 copy-start.2
  1.6 0.6 copy-done.1
  2.2 0.0 copy-done
  2.2 0.0 copy-done.2
  2.2 0.1 pack.1
  2.4 20.1 %all_to_all.30.spg = f32[16,24,128]{2,1,0:T(8,128)S(1)} all-to-all(f32[16,24,128]{2,1,0:T(8,128)S(1)} %get-tuple-element.13), channel_id=1, replica_groups=mesh['x'=4,'z'=8,'y'=4,'c'=2] {'z','c'}, dimensions={0} | all-to-all | bytes 393216 | tf_op jit(solution)/shard_map/all_to_all | solution.py:180
  22.5 19.2 %all_to_all.31.tpg = f32[16,40,256]{2,1,0:T(8,128)S(1)} all-to-all(f32[16,40,256]{2,1,0:T(8,128)S(1)} %get-tuple-element.14), channel_id=1, replica_groups=mesh['x'=4,'z'=8,'y'=4,'c'=2] {'x','y'}, dimensions={0} | all-to-all | bytes 1310720 | tf_op jit(solution)/shard_map/all_to_all | solution.py:180
  41.7 3.6 %row_pass_first.1 = (f32[16,1,1024]{2,1,0:T(1,128)S(1)}, bf16[128,1024]{1,0:T(8,128)(2,1)S(1)}, bf16[128,4096]{1,0:T(8,128)(2,1)S(1)}, f32[1,1024]{1,0:T(1,128)S(1)}, f32[1,4096]{1,0:T(1,128)S(1)}) custom-call(f32[16,24,128]{2,1,0:T(8,128)S(1)} %all_to_all.30.spg, f32[16,40,256]{2,1,0:T(8,128)S(1)} %all_to_all.31.tpg), custom_call_target="tpu_custom_call" | custom-call | tf_op jit(solution)/shard_map/row_pass_first/pallas_call | solution.py:168
  45.3 11.3 %all_to_all.32.parts = f32[16,1,1024]{2,1,0:T(1,128)S(1)} all-to-all(f32[16,1,1024]{2,1,0:T(1,128)S(1)} %get-tuple-element.15), channel_id=1, replica_groups=mesh['x'=4,'z'=8,'y'=4,'c'=2] {'z','c'}, dimensions={0} | all-to-all | bytes 131072 | tf_op jit(solution)/shard_map/all_to_all | solution.py:180
  56.6 3.6 %column_pass.1 = f32[16,1,4096]{2,1,0:T(1,128)S(1)} custom-call(f32[16,1,1024]{2,1,0:T(1,128)S(1)} %all_to_all.32.parts, f32[1,1024]{1,0:T(1,128)S(1)} %get-tuple-element.16.la, bf16[128,1024]{1,0:T(8,128)(2,1)S(1)} %get-tuple-element.17.akm, bf16[128,4096]{1,0:T(8,128)(2,1)S(1)} %get-tuple-element.18.bkm), custom_call_target="tpu_custom_call" | custom-call | tf_op jit(solution)/shard_map/column_pass/pallas_call | solution.py:168
  60.2 10.9 %all_to_all.33.parts = f32[16,1,4096]{2,1,0:T(1,128)S(1)} all-to-all(f32[16,1,4096]{2,1,0:T(1,128)S(1)} %column_pass.1), channel_id=1, replica_groups=mesh['x'=4,'z'=8,'y'=4,'c'=2] {'x','y'}, dimensions={0} | all-to-all | bytes 524288 | tf_op jit(solution)/shard_map/all_to_all | solution.py:180
  71.1 3.8 %row_pass.1 = f32[16,1,1024]{2,1,0:T(1,128)S(1)} custom-call(f32[16,1,4096]{2,1,0:T(1,128)S(1)} %all_to_all.33.parts, f32[1,4096]{1,0:T(1,128)S(1)} %get-tuple-element.19.lb, bf16[128,1024]{1,0:T(8,128)(2,1)S(1)} %get-tuple-element.17.akm, bf16[128,4096]{1,0:T(8,128)(2,1)S(1)} %get-tuple-element.18.bkm), custom_call_target="tpu_custom_call" | custom-call | tf_op jit(solution)/shard_map/row_pass/pallas_call | solution.py:168
  74.9 11.9 %all_to_all.34.parts = f32[16,1,1024]{2,1,0:T(1,128)S(1)} all-to-all(f32[16,1,1024]{2,1,0:T(1,128)S(1)} %row_pass.1), channel_id=1, replica_groups=mesh['x'=4,'z'=8,'y'=4,'c'=2] {'z','c'}, dimensions={0} | all-to-all | bytes 131072 | tf_op jit(solution)/shard_map/all_to_all | solution.py:180
  86.8 4.0 %column_pass_last.1 = (f32[16,1,256]{2,1,0:T(1,128)S(1)}, f32[1,64]{1,0:T(1,128)}) custom-call(f32[16,1,1024]{2,1,0:T(1,128)S(1)} %all_to_all.34.parts, f32[1,1024]{1,0:T(1,128)S(1)} %get-tuple-element.16.la, bf16[128,1024]{1,0:T(8,128)(2,1)S(1)} %get-tuple-element.17.akm, bf16[128,4096]{1,0:T(8,128)(2,1)S(1)} %get-tuple-element.18.bkm, ...), custom_call_target="tpu_custom_call" | custom-call | tf_op jit(solution)/shard_map/column_pass_last/pallas_call | solution.py:168
  90.9 9.6 %all_to_all.35.parts = f32[16,1,256]{2,1,0:T(1,128)S(1)} all-to-all(f32[16,1,256]{2,1,0:T(1,128)S(1)} %get-tuple-element.22), channel_id=1, replica_groups=mesh['x'=4,'z'=8,'y'=4,'c'=2] {'x','y'}, dimensions={0} | all-to-all | bytes 32768 | tf_op jit(solution)/shard_map/all_to_all | solution.py:180
  100.4 0.6 last.1
Async XLA Ops:
  0.6 0.8 copy-start.3
  1.5 0.7 copy-start.1
  1.6 0.7 copy-start
  1.6 0.7 copy-start.2

commit v3 on v2

--- a/solution.py
+++ b/solution.py
@@ -74,53 +74,72 @@
     return write
 
 
-def pack_kernel(src, la, tgt, lb, g, spack, tpack, ssq, tsq):
-    s_t = src[...].T
-    t_t = tgt[...].T
+def pack_kernel(src_hbm, tgt_hbm, lb_hbm, g_hbm, spack, tpack, ssq, tsq, src, tgt, lb, g, sems):
+    pairs = ((src_hbm, src), (tgt_hbm, tgt), (lb_hbm, lb), (g_hbm, g))
+    copies = [pltpu.make_async_copy(a, b, sems.at[i]) for i, (a, b) in enumerate(pairs)]
+    for copy in copies:
+        copy.start()
+    for copy in copies:
+        copy.wait()
+    s_t, t_t = src[...], tgt[...]
     s_norm = jnp.sum(s_t * s_t, axis=0, keepdims=True)
     t_norm = jnp.sum(t_t * t_t, axis=0, keepdims=True)
     ssq[...] = s_norm
     tsq[...] = t_norm
     s_t = s_t * ((2.0 / EPSILON) * LOG2E)
+    packed = jnp.concatenate([s_t[: DIM // 2], s_t[DIM // 2 :]], axis=1)
+    spack[...] = packed
+    h = (lb[...] + (g[...] - t_norm) / EPSILON) * LOG2E
+    weights = lb[...] * LOG2E
+    half = t_t.shape[1] // 2
+    rows = [t_t[:, :half], t_t[:, half:], h[:, :half], h[:, half:], weights[:, :half], weights[:, half:]]
+    packed = jnp.concatenate(rows + [jnp.zeros((4, half), F32)], axis=0)
+    tpack[...] = jnp.broadcast_to(packed[None], tpack.shape)
+
+
+def first_kernel(group0, group2, group4, group6, tpg, la, out, akm, bkm, lb, brm, bh, packs):
+    own = la.shape[1]
     half = DIM // 2
-    weights = jnp.concatenate([la[...] * LOG2E, jnp.zeros_like(la[...])], axis=1)
-    packed = jnp.concatenate(
-        [jnp.concatenate([s_t[:half], s_t[half:]], axis=1), jnp.broadcast_to(weights, (8, weights.shape[1]))], axis=0
-    )
-    spack[...] = jnp.broadcast_to(packed[None], spack.shape)
-    h = (lb[...] + (g[...] - t_norm) / EPSILON) * LOG2E
-    rest = jnp.concatenate([h, lb[...] * LOG2E, jnp.zeros((6, h.shape[1]), F32)], axis=0)
-    tpack[...] = jnp.broadcast_to(jnp.concatenate([t_t, rest], axis=0)[None], tpack.shape)
-
-
-def first_kernel(spg, tpg, out, akm, bkm, la, lb, brm, bh):
-    groups, _, lanes = spg.shape
-    half = DIM // 2
-    own = lanes // 2
+    me = lax.axis_index(TARGET_AXES)
+    groups = (group0, group2, group4, group6)
+    for p in range(packs.shape[0]):
+        packs[p] = groups[p // 4][half * (p % 4) : half * (p % 4 + 1)]
     pieces = []
-    for p in range(0, groups, 2):
-        a, b = spg[p], spg[p + 1]
+    for p in range(0, packs.shape[0], 2):
+        a, b = packs[p ^ me], packs[(p + 1) ^ me]
         top = jnp.concatenate([a[:, :own], b[:, :own]], axis=1)
-        low = jnp.concatenate([a[:half, own:], b[:half, own:]], axis=1)
-        la[:, own * p : own * (p + 2)] = top[half : half + 1]
-        pieces.append(jnp.concatenate([top[:half], low], axis=0))
+        low = jnp.concatenate([a[:, own:], b[:, own:]], axis=1)
+        pieces.append(jnp.concatenate([top, low], axis=0))
     s = jnp.concatenate(pieces, axis=1)
     s1, s2 = (v.astype(BF16) for v in split(s, 2))
     width = s.shape[1]
     none = jnp.zeros((1, width), F32)
     akm[...] = jnp.concatenate([s1, s1, s2, vector_rows(none, None, width), jnp.zeros((16, width), BF16)], axis=0)
-    width = tpg.shape[2]
+    weights = jnp.concatenate([la[...] * LOG2E, jnp.zeros_like(la[...])], axis=1)
+    out[:, :, width:] = jnp.broadcast_to(weights[None], (out.shape[0], 1, 2 * own))
+    width = 2 * tpg.shape[2]
     none = jnp.zeros((1, width), F32)
+    zeros = jnp.zeros((16, width), BF16)
     for p in range(tpg.shape[0]):
         at = slice(width * p, width * (p + 1))
-        t1, t2 = (v.astype(BF16) for v in split(tpg[p, :DIM], 2))
-        h = tpg[p, DIM : DIM + 1]
-        lb[:, at] = tpg[p, DIM + 1 : DIM + 2]
-        zeros = jnp.zeros((16, width), BF16)
+        wide = lambda row, count: jnp.concatenate([tpg[p, row : row + count], tpg[p, row + count : row + 2 * count]], axis=1)
+        t1, t2 = (v.astype(BF16) for v in split(wide(0, DIM), 2))
+        h = wide(2 * DIM, 1)
+        lb[:, at] = wide(2 * DIM + 2, 1)
         bkm[:, at] = jnp.concatenate([t1, t2, t1, vector_rows(None, none, width), zeros], axis=0)
         bh[...] = jnp.concatenate([t1, t2, t1, vector_rows(None, h, width), zeros], axis=0)
         brm[at, :] = bh[...].T
     lse_pass(brm, akm, write_copies(out))
+
+
+def first_column_kernel(parts, akm, bkm, out, la, arm, tmp):
+    rows = la.shape[1]
+    own = rows // parts.shape[0]
+    for p in range(0, parts.shape[0], 2):
+        la[:, own * p : own * (p + 2)] = jnp.concatenate(
+            [parts[p, :, rows : rows + own], parts[p + 1, :, rows : rows + own]], axis=1
+        )
+    column_kernel(parts.at[:, :, :rows], la, akm, bkm, out, arm, tmp)
 
 
 def column_kernel(parts, la, akm, bkm, out, arm, tmp):
@@ -163,13 +182,13 @@
     g[...] = tsq[...] - (EPSILON * LN2) * combine(parts[...])
 
 
-def call(kernel, name, outs, *args, scratch=()):
+def call(kernel, name, outs, *args, scratch=(), inputs=pltpu.VMEM):
     whole = pl.BlockSpec(memory_space=pltpu.VMEM)
     return pl.pallas_call(
         kernel,
         name=name,
         out_shape=[jax.ShapeDtypeStruct(*o) for o in outs],
-        in_specs=[whole] * len(args),
+        in_specs=[pl.BlockSpec(memory_space=inputs)] * len(args),
         out_specs=[whole] * len(outs),
         scratch_shapes=list(scratch),
         compiler_params=PARAMS,
@@ -178,6 +197,11 @@
 
 def exchange(v, axes):
     return lax.all_to_all(v, axes, 0, 0, tiled=True)
+
+
+def swap(v, axis, offset):
+    size = lax.axis_size(axis)
+    return lax.ppermute(v, axis, [(i, i ^ offset) for i in range(size)])
 
 
 def local(src_points, log_a, tgt_points, log_b, g_init):
@@ -190,33 +214,39 @@
         pack_kernel,
         "pack",
         [
-            ((across_t, DIM // 2 + 8, 2 * own_s), F32),
-            ((across_s, DIM + 8, own_t), F32),
+            ((DIM // 2, 2 * own_s), F32),
+            ((across_s, 2 * DIM + 8, own_t // 2), F32),
             ((1, own_s), F32),
             ((1, own_t), F32),
         ],
-        src_points,
-        row(log_a),
-        tgt_points,
-        row(log_b),
-        row(g_init),
-    )
-    spg = exchange(spack, TARGET_AXES)
+        *(pltpu.with_memory_space_constraint(v, pltpu.HBM) for v in (src_points.T, tgt_points.T, row(log_b), row(g_init))),
+        scratch=[pltpu.VMEM((DIM, own_s), F32), pltpu.VMEM((DIM, own_t), F32)]
+        + [pltpu.VMEM((1, own_t), F32)] * 2
+        + [pltpu.SemaphoreType.DMA((4,))],
+        inputs=pltpu.HBM,
+    )
+    group = jnp.concatenate([spack, swap(spack, "c", 1)], axis=0)
+    group = jnp.concatenate([group, swap(group, "z", 1)], axis=0)
+    groups = [group] + [swap(group, "z", k) for k in (2, 4, 6)]
     tpg = exchange(tpack, SOURCE_AXES)
     row_out = ((across_t, 1, rows), F32)
     col_out = ((across_s, 1, cols), F32)
-    parts, akm, bkm, la, lb = call(
+    parts, akm, bkm, lb = call(
         first_kernel,
         "row_pass_first",
-        [row_out, ((DEPTH, rows), BF16), ((DEPTH, cols), BF16), ((1, rows), F32), ((1, cols), F32)],
-        spg,
+        [((across_t, 1, rows + 2 * own_s), F32), ((DEPTH, rows), BF16), ((DEPTH, cols), BF16), ((1, cols), F32)],
+        *groups,
         tpg,
-        scratch=[pltpu.VMEM((cols, DEPTH), BF16), pltpu.VMEM((DEPTH, own_t), BF16)],
+        row(log_a),
+        scratch=[pltpu.VMEM((cols, DEPTH), BF16), pltpu.VMEM((DEPTH, own_t), BF16)]
+        + [pltpu.VMEM((across_t, DIM // 2, 2 * own_s), F32)],
     )
     row_scratch = [pltpu.VMEM((cols, DEPTH), BF16), pltpu.VMEM((DEPTH, cols), BF16)]
     col_scratch = [pltpu.VMEM((rows, DEPTH), BF16), pltpu.VMEM((DEPTH, rows), BF16)]
     parts = exchange(parts, TARGET_AXES)
-    (parts,) = call(column_kernel, "column_pass", [col_out], parts, la, akm, bkm, scratch=col_scratch)
+    parts, la = call(
+        first_column_kernel, "column_pass", [col_out, ((1, rows), F32)], parts, akm, bkm, scratch=col_scratch
+    )
     parts = exchange(parts, SOURCE_AXES)
     (parts,) = call(row_kernel, "row_pass", [row_out], parts, lb, akm, bkm, scratch=row_scratch)
     parts = exchange(parts, TARGET_AXES)

time: 101 us -> 93.9 us (0.930)
  blocking collectives: 83 us -> 50.2 us
  starting transfers between devices: 0 us -> 18.5 us
  waiting for transfers between devices: 0 us -> 6.97 us
  local copies, waits for them, and re-layouts: 1.58 us -> 0.01 us
  Pallas kernels: 15.8 us -> 17.2 us
    all_to_all x6 -> x4, blocking collectives: 83 us -> 50.2 us  [exchange(): return lax.all_to_all(v, axes, 0, 0, tiled=True)]
    ppermute x0 -> x5, starting transfers between devices: none -> 10.9 us  [swap(): return lax.ppermute(v, axis, [(i, i ^ offset) for i in range(size)])]
    all_to_all x0 -> x1, starting transfers between devices: none -> 7.6 us  [exchange(): return lax.all_to_all(v, axes, 0, 0, tiled=True)]
    ppermute x0 -> x5, waiting for transfers between devices: none -> 6.97 us  [swap(): return lax.ppermute(v, axis, [(i, i ^ offset) for i in range(size)])]
    unnamed x10 -> x4, local copies, waits for them, and re-layouts: 1.58 us -> 0.01 us
    pallas_call x6, Pallas kernels: 15.8 us -> 17.2 us  [call(): pl.pallas_call(kernel, name=name, out_shape=[jax.ShapeDtypeStruct(*o) for...]
  transfers between devices with their start and end apart: 0 -> 6, of which waited for: 0 -> 3; matrix products, arithmetic and copies ran while one was open for 0% -> 0% of each run, Pallas kernels for 0% -> 0%
where the time goes in v3:
time: 93.9 us; the launch traced here: 93.5 us
  blocking collectives  50.2 us (53%)
  starting transfers between devices  18.5 us (20%)
  Pallas kernels  17.2 us (18%)
  waiting for transfers between devices  6.97 us (7%)
    all_to_all x4, blocking collectives, exchange(): return lax.all_to_all(v, axes, 0, 0, tiled=True)  50.2 us
    pallas_call x6, Pallas kernels, call(): pl.pallas_call(kernel, name=name, out_shape=[jax.ShapeDtypeStruct(*o) for...  17.2 us
    ppermute x5, starting transfers between devices, swap(): return lax.ppermute(v, axis, [(i, i ^ offset) for i in range(size)])  10.9 us
    all_to_all x1, starting transfers between devices, exchange(): return lax.all_to_all(v, axes, 0, 0, tiled=True)  7.6 us
    ppermute x5, waiting for transfers between devices, swap(): return lax.ppermute(v, axis, [(i, i ^ offset) for i in range(size)])  6.97 us
  transfers between devices with their start and end apart: 6, of which 3 were waited for; matrix products, arithmetic and copies ran while one was open for 0% of the time, Pallas kernels for 0%

profile of v3, /device:TPU:1, one launch (start us, length us, event | category | flops | bytes accessed | tf_op | source)
XLA Modules:
  0.0 93.5 jit_solution(1283760869590724889)
XLA Ops:
  0.6 1.7 %pack.1 = (f32[16,128]{1,0:T(8,128)S(1)}, f32[16,72,128]{2,1,0:T(8,128)}, f32[1,64]{1,0:T(1,128)S(1)}, f32[1,256]{1,0:T(1,128)S(1)}) custom-call(f32[32,64]{1,0:T(8,128)} %bitcast.9, f32[32,256]{1,0:T(8,128)} %bitcast.8, f32[1,256]{1,0:T(1,128)} %bitcast.10, f32[1,256]{1,0:T(1,128)} %bitcast.11), custom_call_target="tpu_custom_call" | custom-call | tf_op jit(solution)/shard_map/pack/pallas_call | solution.py:187
  2.3 7.6 %all-to-all-start = ((f32[16,72,128]{2,1,0:T(8,128)}), f32[16,72,128]{2,1,0:T(8,128)S(1)}, u32[]{:S(2)}, u32[]{:S(2)}) async-start(f32[16,72,128]{2,1,0:T(8,128)} %get-tuple-element.15), calls=%async_computation | async-start | bytes 1179648 | tf_op jit(solution)/shard_map/all_to_all | solution.py:199
  9.9 1.0 %collective-permute-start = (f32[16,128]{1,0:T(8,128)S(1)}, f32[16,128]{1,0:T(8,128)S(1)}, u32[]{:S(2)}, u32[]{:S(2)}) collective-permute-start(f32[16,128]{1,0:T(8,128)S(1)} %get-tuple-element.14), channel_id=1, source_target_pairs={{0,1},{1,0},{2,3},{3,2},{4,5},{5,4},{6,7},{7,6},{8,9},{9,8},{10,11... | collective-permute-start | bytes 24584 | tf_op jit(solution)/shard_map/ppermute | solution.py:204
  10.9 0.8 collective-permute-done
  11.8 1.6 %collective-permute-start.1 = (f32[32,128]{1,0:T(8,128)S(1)}, f32[32,128]{1,0:T(8,128)S(1)}, u32[]{:S(2)}, u32[]{:S(2)}) collective-permute-start(f32[32,128]{1,0:T(8,128)S(1)} %pad_maximum_fusion), channel_id=1, source_target_pairs={{0,8},{8,0},{16,24},{24,16},{32,40},{40,32},{48,56},{56,48},{1,9},... | collective-permute-start | bytes 49160 | tf_op jit(solution)/shard_map/ppermute | solution.py:204
  13.4 1.1 %collective-permute-done.1 = f32[32,128]{1,0:T(8,128)S(1)} collective-permute-done((f32[32,128]{1,0:T(8,128)S(1)}, f32[32,128]{1,0:T(8,128)S(1)}, u32[]{:S(2)}, u32[]{:S(2)}) %collective-permute-start.1) | collective-permute-done | bytes 16416 | tf_op jit(solution)/shard_map/ppermute | solution.py:204
  14.5 0.0 copy-start
  14.5 6.0 %collective-permute-start.4 = (f32[64,128]{1,0:T(8,128)S(1)}, f32[64,128]{1,0:T(8,128)S(1)}, u32[]{:S(2)}, u32[]{:S(2)}) collective-permute-start(f32[64,128]{1,0:T(8,128)S(1)} %constant_dynamic-update-slice_fusion.group0), channel_id=1, source_target_pairs={{0,48},{8,56},{16,32},{24,40},{32,16},{40,24},{48,0},{56,8},{1,49}... | collective-permute-start | bytes 98312 | tf_op jit(solution)/shard_map/ppermute | solution.py:204
  20.6 1.0 %collective-permute-start.3 = (f32[64,128]{1,0:T(8,128)S(1)}, f32[64,128]{1,0:T(8,128)S(1)}, u32[]{:S(2)}, u32[]{:S(2)}) collective-permute-start(f32[64,128]{1,0:T(8,128)S(1)} %constant_dynamic-update-slice_fusion.group0), channel_id=1, source_target_pairs={{0,32},{8,40},{16,48},{24,56},{32,0},{40,8},{48,16},{56,24},{1,33}... | collective-permute-start | bytes 98312 | tf_op jit(solution)/shard_map/ppermute | solution.py:204
  21.5 1.2 %collective-permute-start.2 = (f32[64,128]{1,0:T(8,128)S(1)}, f32[64,128]{1,0:T(8,128)S(1)}, u32[]{:S(2)}, u32[]{:S(2)}) collective-permute-start(f32[64,128]{1,0:T(8,128)S(1)} %constant_dynamic-update-slice_fusion.group0), channel_id=1, source_target_pairs={{0,16},{8,24},{16,0},{24,8},{32,48},{40,56},{48,32},{56,40},{1,17}... | collective-permute-start | bytes 98312 | tf_op jit(solution)/shard_map/ppermute | solution.py:204
  22.7 0.0 collective-permute-done.4.group6
  22.7 5.0 %collective-permute-done.3.group4 = f32[64,128]{1,0:T(8,128)S(1)} collective-permute-done((f32[64,128]{1,0:T(8,128)S(1)}, f32[64,128]{1,0:T(8,128)S(1)}, u32[]{:S(2)}, u32[]{:S(2)}) %collective-permute-start.3) | collective-permute-done | bytes 32800 | tf_op jit(solution)/shard_map/ppermute | solution.py:204
  27.8 0.0 collective-permute-done.2.group2
  27.8 0.0 all-to-all-done.tpg
  27.8 0.0 copy-done
  27.8 3.5 %row_pass_first.1 = (f32[16,1,1152]{2,1,0:T(1,128)S(1)}, bf16[128,1024]{1,0:T(8,128)(2,1)S(1)}, bf16[128,4096]{1,0:T(8,128)(2,1)S(1)}, f32[1,4096]{1,0:T(1,128)S(1)}) custom-call(f32[64,128]{1,0:T(8,128)S(1)} %constant_dynamic-update-slice_fusion.group0, f32[64,128]{1,0:T(8,128)S(1)} %collective-permute-done.2.group2, ...), custom_call_target="tpu_custom_call" | custom-call | tf_op jit(solution)/shard_map/row_pass_first/pallas_call | solution.py:187
  31.3 14.2 %all_to_all.25.parts = f32[16,1,1152]{2,1,0:T(1,128)S(1)} all-to-all(f32[16,1,1152]{2,1,0:T(1,128)S(1)} %get-tuple-element.16), channel_id=1, replica_groups=mesh['x'=4,'z'=8,'y'=4,'c'=2] {'z','c'}, dimensions={0} | all-to-all | bytes 147456 | tf_op jit(solution)/shard_map/all_to_all | solution.py:199
  45.5 3.6 %column_pass.1 = (f32[16,1,4096]{2,1,0:T(1,128)S(1)}, f32[1,1024]{1,0:T(1,128)S(1)}) custom-call(f32[16,1,1152]{2,1,0:T(1,128)S(1)} %all_to_all.25.parts, bf16[128,1024]{1,0:T(8,128)(2,1)S(1)} %get-tuple-element.17.akm, bf16[128,4096]{1,0:T(8,128)(2,1)S(1)} %get-tuple-element.18.bkm), custom_call_target="tpu_custom_call" | custom-call | tf_op jit(solution)/shard_map/column_pass/pallas_call | solution.py:187
  49.1 14.4 %all_to_all.26.parts = f32[16,1,4096]{2,1,0:T(1,128)S(1)} all-to-all(f32[16,1,4096]{2,1,0:T(1,128)S(1)} %get-tuple-element.19), channel_id=1, replica_groups=mesh['x'=4,'z'=8,'y'=4,'c'=2] {'x','y'}, dimensions={0} | all-to-all | bytes 524288 | tf_op jit(solution)/shard_map/all_to_all | solution.py:199
  63.5 3.9 %row_pass.1 = f32[16,1,1024]{2,1,0:T(1,128)S(1)} custom-call(f32[16,1,4096]{2,1,0:T(1,128)S(1)} %all_to_all.26.parts, f32[1,4096]{1,0:T(1,128)S(1)} %get-tuple-element.20.lb, bf16[128,1024]{1,0:T(8,128)(2,1)S(1)} %get-tuple-element.17.akm, bf16[128,4096]{1,0:T(8,128)(2,1)S(1)} %get-tuple-element.18.bkm), custom_call_target="tpu_custom_call" | custom-call | tf_op jit(solution)/shard_map/row_pass/pallas_call | solution.py:187
  67.3 12.0 %all_to_all.27.parts = f32[16,1,1024]{2,1,0:T(1,128)S(1)} all-to-all(f32[16,1,1024]{2,1,0:T(1,128)S(1)} %row_pass.1), channel_id=1, replica_groups=mesh['x'=4,'z'=8,'y'=4,'c'=2] {'z','c'}, dimensions={0} | all-to-all | bytes 131072 | tf_op jit(solution)/shard_map/all_to_all | solution.py:199
  79.3 4.0 %column_pass_last.1 = (f32[16,1,256]{2,1,0:T(1,128)S(1)}, f32[1,64]{1,0:T(1,128)}) custom-call(f32[16,1,1024]{2,1,0:T(1,128)S(1)} %all_to_all.27.parts, f32[1,1024]{1,0:T(1,128)S(1)} %get-tuple-element.21.la, bf16[128,1024]{1,0:T(8,128)(2,1)S(1)} %get-tuple-element.17.akm, bf16[128,4096]{1,0:T(8,128)(2,1)S(1)} %get-tuple-element.18.bkm, ...), custom_call_target="tpu_custom_call" | custom-call | tf_op jit(solution)/shard_map/column_pass_last/pallas_call | solution.py:187
  83.3 9.6 %all_to_all.28.parts = f32[16,1,256]{2,1,0:T(1,128)S(1)} all-to-all(f32[16,1,256]{2,1,0:T(1,128)S(1)} %get-tuple-element.24), channel_id=1, replica_groups=mesh['x'=4,'z'=8,'y'=4,'c'=2] {'x','y'}, dimensions={0} | all-to-all | bytes 32768 | tf_op jit(solution)/shard_map/all_to_all | solution.py:199
  92.9 0.6 last.1
  (4 shorter events, 0.0 us)
Async XLA Ops:
  2.3 25.5 %all-to-all-start = ((f32[16,72,128]{2,1,0:T(8,128)}), f32[16,72,128]{2,1,0:T(8,128)S(1)}, u32[]{:S(2)}, u32[]{:S(2)}) async-start(f32[16,72,128]{2,1,0:T(8,128)} %get-tuple-element.15), calls=%async_computation | async-start | bytes 1179648 | tf_op jit(solution)/shard_map/all_to_all | solution.py:199
  9.9 1.9 %collective-permute-start = (f32[16,128]{1,0:T(8,128)S(1)}, f32[16,128]{1,0:T(8,128)S(1)}, u32[]{:S(2)}, u32[]{:S(2)}) collective-permute-start(f32[16,128]{1,0:T(8,128)S(1)} %get-tuple-element.14), channel_id=1, source_target_pairs={{0,1},{1,0},{2,3},{3,2},{4,5},{5,4},{6,7},{7,6},{8,9},{9,8},{10,11... | collective-permute-start | bytes 24584 | tf_op jit(solution)/shard_map/ppermute | solution.py:204
  11.8 2.8 %collective-permute-start.1 = (f32[32,128]{1,0:T(8,128)S(1)}, f32[32,128]{1,0:T(8,128)S(1)}, u32[]{:S(2)}, u32[]{:S(2)}) collective-permute-start(f32[32,128]{1,0:T(8,128)S(1)} %pad_maximum_fusion), channel_id=1, source_target_pairs={{0,8},{8,0},{16,24},{24,16},{32,40},{40,32},{48,56},{56,48},{1,9},... | collective-permute-start | bytes 49160 | tf_op jit(solution)/shard_map/ppermute | solution.py:204
  14.5 13.2 %copy-start = (f32[64]{0:T(128)S(1)}, f32[64]{0:T(128)}, u32[]{:S(2)}) copy-start(f32[64]{0:T(128)} %param.6) | copy-start | bytes 772
  14.5 8.2 %collective-permute-start.4 = (f32[64,128]{1,0:T(8,128)S(1)}, f32[64,128]{1,0:T(8,128)S(1)}, u32[]{:S(2)}, u32[]{:S(2)}) collective-permute-start(f32[64,128]{1,0:T(8,128)S(1)} %constant_dynamic-update-slice_fusion.group0), channel_id=1, source_target_pairs={{0,48},{8,56},{16,32},{24,40},{32,16},{40,24},{48,0},{56,8},{1,49}... | collective-permute-start | bytes 98312 | tf_op jit(solution)/shard_map/ppermute | solution.py:204
  20.6 7.2 %collective-permute-start.3 = (f32[64,128]{1,0:T(8,128)S(1)}, f32[64,128]{1,0:T(8,128)S(1)}, u32[]{:S(2)}, u32[]{:S(2)}) collective-permute-start(f32[64,128]{1,0:T(8,128)S(1)} %constant_dynamic-update-slice_fusion.group0), channel_id=1, source_target_pairs={{0,32},{8,40},{16,48},{24,56},{32,0},{40,8},{48,16},{56,24},{1,33}... | collective-permute-start | bytes 98312 | tf_op jit(solution)/shard_map/ppermute | solution.py:204
  21.5 6.2 %collective-permute-start.2 = (f32[64,128]{1,0:T(8,128)S(1)}, f32[64,128]{1,0:T(8,128)S(1)}, u32[]{:S(2)}, u32[]{:S(2)}) collective-permute-start(f32[64,128]{1,0:T(8,128)S(1)} %constant_dynamic-update-slice_fusion.group0), channel_id=1, source_target_pairs={{0,16},{8,24},{16,0},{24,8},{32,48},{40,56},{48,32},{56,40},{1,17}... | collective-permute-start | bytes 98312 | tf_op jit(solution)/shard_map/ppermute | solution.py:204

commit v4 on v3

--- a/solution.py
+++ b/solution.py
@@ -18,11 +18,12 @@
 DIM = 32
 DEPTH = 128
 VEC = 3 * DIM
-TILE = 512
+TILE = 256
 CHUNK = 128
+OVERFLOW = 1e38
 F32 = jnp.float32
 BF16 = jnp.bfloat16
-PARAMS = pltpu.CompilerParams(vmem_limit_bytes=48 << 20)
+JOIN_COST = pl.CostEstimate(flops=1000000000000, bytes_accessed=0, transcendentals=0)
 
 
 def split(v, count):
@@ -50,26 +51,52 @@
 
 
 def lse_pass(lhs_ref, rhs_ref, write):
+    largest = None
     for at in range(0, rhs_ref.shape[1], TILE):
         rhs = rhs_ref[:, at : at + TILE]
         top = total = None
         for row in range(0, lhs_ref.shape[0], CHUNK):
             terms = jnp.dot(lhs_ref[row : row + CHUNK, :], rhs, preferred_element_type=F32)
             terms = terms.reshape(CHUNK // 8, 8, TILE)
-            newtop = jnp.max(terms, axis=0)
-            if top is not None:
-                newtop = jnp.maximum(top, newtop)
+            if top is None:
+                top = jnp.max(jnp.max(terms, axis=0), axis=0, keepdims=True)
+            added = jnp.sum(jnp.exp2(terms - top[None]), axis=0)
+            total = added if total is None else total + added
+        total = jnp.sum(total, axis=0, keepdims=True)
+        largest = total if largest is None else jnp.maximum(largest, total)
+        write(at // TILE, top + jnp.log2(total))
+
+    @pl.when(jnp.logical_not(jnp.max(largest) < OVERFLOW))
+    def _():
+        running_lse_pass(lhs_ref, rhs_ref, write)
+
+
+def running_lse_pass(lhs_ref, rhs_ref, write):
+    def tile(n, carry):
+        rhs = rhs_ref[:, pl.ds(pl.multiple_of(n * TILE, TILE), TILE)]
+
+        def step(r, state):
+            top, total = state
+            lhs = lhs_ref[pl.ds(pl.multiple_of(r * CHUNK, CHUNK), CHUNK), :]
+            terms = jnp.dot(lhs, rhs, preferred_element_type=F32).reshape(CHUNK // 8, 8, TILE)
+            newtop = jnp.maximum(top, jnp.max(terms, axis=0))
             added = jnp.sum(jnp.exp2(terms - newtop[None]), axis=0)
-            total = added if top is None else total * jnp.exp2(top - newtop) + added
-            top = newtop
+            return newtop, total * jnp.exp2(top - newtop) + added
+
+        start = (jnp.full((8, TILE), -1e30, F32), jnp.zeros((8, TILE), F32))
+        top, total = lax.fori_loop(0, lhs_ref.shape[0] // CHUNK, step, start, unroll=8)
         peak = jnp.max(top, axis=0, keepdims=True)
         total = jnp.sum(total * jnp.exp2(top - peak), axis=0, keepdims=True)
-        write(at, peak + jnp.log2(total))
+        write(n, peak + jnp.log2(total))
+        return carry
+
+    lax.fori_loop(0, rhs_ref.shape[1] // TILE, tile, 0)
 
 
 def write_copies(out_ref):
-    def write(at, value):
-        out_ref[:, :, at : at + TILE] = jnp.broadcast_to(value[None], (out_ref.shape[0], 1, TILE))
+    def write(n, value):
+        at = pl.ds(n * TILE if isinstance(n, int) else pl.multiple_of(n * TILE, TILE), TILE)
+        out_ref[:, :, at] = jnp.broadcast_to(value[None], (out_ref.shape[0], 1, TILE))
 
     return write
 
@@ -97,13 +124,20 @@
     tpack[...] = jnp.broadcast_to(packed[None], tpack.shape)
 
 
-def first_kernel(group0, group2, group4, group6, tpg, la, out, akm, bkm, lb, brm, bh, packs):
+def join_kernel(first, second, out):
+    rows = first.shape[0]
+    out[:rows] = first[...]
+    out[rows:] = second[...]
+
+
+def first_kernel(even, odd, even_c, odd_c, tpg, la, out, akm, bkm, lb, brm, bh, packs):
     own = la.shape[1]
     half = DIM // 2
     me = lax.axis_index(TARGET_AXES)
-    groups = (group0, group2, group4, group6)
-    for p in range(packs.shape[0]):
-        packs[p] = groups[p // 4][half * (p % 4) : half * (p % 4 + 1)]
+    for at, offset in enumerate((0, 4, 2, 6)):
+        row = slice(half * at, half * (at + 1))
+        for other, group in enumerate((even, even_c, odd, odd_c)):
+            packs[2 * offset + other] = group[row]
     pieces = []
     for p in range(0, packs.shape[0], 2):
         a, b = packs[p ^ me], packs[(p + 1) ^ me]
@@ -171,9 +205,8 @@
     tmp[VEC : VEC + 16, :] = vector_rows(k, None, k.shape[1])
     arm[...] = tmp[...].T
 
-    def write(at, value):
-        for own in range(0, TILE, out.shape[2]):
-            out[(at + own) // out.shape[2]] = value[:, own : own + out.shape[2]]
+    def write(n, value):
+        out[n] = value
 
     lse_pass(arm, bkm, write)
 
@@ -182,7 +215,7 @@
     g[...] = tsq[...] - (EPSILON * LN2) * combine(parts[...])
 
 
-def call(kernel, name, outs, *args, scratch=(), inputs=pltpu.VMEM):
+def call(kernel, name, outs, *args, scratch=(), inputs=pltpu.VMEM, cost=None, vmem=48):
     whole = pl.BlockSpec(memory_space=pltpu.VMEM)
     return pl.pallas_call(
         kernel,
@@ -191,7 +224,8 @@
         in_specs=[pl.BlockSpec(memory_space=inputs)] * len(args),
         out_specs=[whole] * len(outs),
         scratch_shapes=list(scratch),
-        compiler_params=PARAMS,
+        compiler_params=pltpu.CompilerParams(vmem_limit_bytes=vmem << 20),
+        cost_estimate=cost,
     )(*args)
 
 
@@ -224,10 +258,14 @@
         + [pltpu.VMEM((1, own_t), F32)] * 2
         + [pltpu.SemaphoreType.DMA((4,))],
         inputs=pltpu.HBM,
-    )
-    group = jnp.concatenate([spack, swap(spack, "c", 1)], axis=0)
-    group = jnp.concatenate([group, swap(group, "z", 1)], axis=0)
-    groups = [group] + [swap(group, "z", k) for k in (2, 4, 6)]
+        vmem=8,
+    )
+    pair = call(
+        join_kernel, "join", [((DIM, 2 * own_s), F32)], spack, swap(spack, "z", 4), cost=JOIN_COST, vmem=2
+    )[0]
+    even = jnp.concatenate([pair, swap(pair, "z", 2)], axis=0)
+    odd = swap(even, "z", 1)
+    groups = [even, odd, swap(even, "c", 1), swap(odd, "c", 1)]
     tpg = exchange(tpack, SOURCE_AXES)
     row_out = ((across_t, 1, rows), F32)
     col_out = ((across_s, 1, cols), F32)

time: 93.9 us -> 97.5 us (1.038)
  Pallas kernels: 17.2 us -> 27.7 us
  blocking collectives: 50.2 us -> 44 us
  starting transfers between devices: 18.5 us -> 22.2 us
  waiting for transfers between devices: 6.97 us -> 3.44 us
    pallas_call x6 -> x7, Pallas kernels: 17.2 us -> 27.7 us  [call(): pl.pallas_call(kernel, name=name, out_shape=[jax.ShapeDtypeStruct(*o) for...]
    all_to_all x4, blocking collectives: 50.2 us -> 44 us  [exchange(): return lax.all_to_all(v, axes, 0, 0, tiled=True)]
    ppermute x5, starting transfers between devices: 10.9 us -> 15.4 us  [swap(): return lax.ppermute(v, axis, [(i, i ^ offset) for i in range(size)])]
    ppermute x5, waiting for transfers between devices: 6.97 us -> 3.16 us  [swap(): return lax.ppermute(v, axis, [(i, i ^ offset) for i in range(size)])]
where the time goes in v4:
time: 97.5 us; the launch traced here: 98 us
  blocking collectives  44 us (45%)
  Pallas kernels  27.7 us (28%)
  starting transfers between devices  22.2 us (23%)
  waiting for transfers between devices  3.44 us (4%)
    all_to_all x4, blocking collectives, exchange(): return lax.all_to_all(v, axes, 0, 0, tiled=True)  44 us
    pallas_call x7, Pallas kernels, call(): pl.pallas_call(kernel, name=name, out_shape=[jax.ShapeDtypeStruct(*o) for...  27.7 us
    ppermute x5, starting transfers between devices, swap(): return lax.ppermute(v, axis, [(i, i ^ offset) for i in range(size)])  15.4 us
    all_to_all x1, starting transfers between devices, exchange(): return lax.all_to_all(v, axes, 0, 0, tiled=True)  6.8 us
    ppermute x5, waiting for transfers between devices, swap(): return lax.ppermute(v, axis, [(i, i ^ offset) for i in range(size)])  3.16 us
  transfers between devices with their start and end apart: 6, of which 3 were waited for; matrix products, arithmetic and copies ran while one was open for 0% of the time, Pallas kernels for 0%

profile of v4, /device:TPU:1, one launch (start us, length us, event | category | flops | bytes accessed | tf_op | source)
XLA Modules:
  0.0 98.0 jit_solution(12623342568430109549)
XLA Ops:
  0.6 1.7 %pack.1 = (f32[16,128]{1,0:T(8,128)S(1)}, f32[16,72,128]{2,1,0:T(8,128)}, f32[1,64]{1,0:T(1,128)S(1)}, f32[1,256]{1,0:T(1,128)S(1)}) custom-call(f32[32,64]{1,0:T(8,128)} %bitcast.9, f32[32,256]{1,0:T(8,128)} %bitcast.8, f32[1,256]{1,0:T(1,128)} %bitcast.10, f32[1,256]{1,0:T(1,128)} %bitcast.11), custom_call_target="tpu_custom_call" | custom-call | tf_op jit(solution)/shard_map/pack/pallas_call | solution.py:220
  2.3 7.8 %collective-permute-start = (f32[16,128]{1,0:T(8,128)S(1)}, f32[16,128]{1,0:T(8,128)S(1)}, u32[]{:S(2)}, u32[]{:S(2)}) collective-permute-start(f32[16,128]{1,0:T(8,128)S(1)} %get-tuple-element.14.first), channel_id=1, source_target_pairs={{0,32},{8,40},{16,48},{24,56},{32,0},{40,8},{48,16},{56,24},{1,33}... | collective-permute-start | bytes 24584 | tf_op jit(solution)/shard_map/ppermute | solution.py:238
  10.1 6.8 %all-to-all-start = ((f32[16,72,128]{2,1,0:T(8,128)}), f32[16,72,128]{2,1,0:T(8,128)}, u32[]{:S(2)}, u32[]{:S(2)}) async-start(f32[16,72,128]{2,1,0:T(8,128)} %get-tuple-element.15), calls=%async_computation | async-start | bytes 1179648 | tf_op jit(solution)/shard_map/all_to_all | solution.py:233
  16.9 0.0 collective-permute-done.second
  17.0 1.3 %collective-permute-start.1 = (f32[32,128]{1,0:T(8,128)S(1)}, f32[32,128]{1,0:T(8,128)S(1)}, u32[]{:S(2)}, u32[]{:S(2)}) collective-permute-start(f32[32,128]{1,0:T(8,128)S(1)} %join.1), channel_id=1, source_target_pairs={{0,16},{8,24},{16,0},{24,8},{32,48},{40,56},{48,32},{56,40},{1,17}... | collective-permute-start | bytes 49160 | tf_op jit(solution)/shard_map/ppermute | solution.py:238
  18.2 2.3 %collective-permute-done.1 = f32[32,128]{1,0:T(8,128)S(1)} collective-permute-done((f32[32,128]{1,0:T(8,128)S(1)}, f32[32,128]{1,0:T(8,128)S(1)}, u32[]{:S(2)}, u32[]{:S(2)}) %collective-permute-start.1) | collective-permute-done | bytes 16416 | tf_op jit(solution)/shard_map/ppermute | solution.py:238
  20.5 0.0 copy-start
  20.5 0.7 collective-permute-start.2
  21.3 2.7 %collective-permute-start.3 = (f32[64,128]{1,0:T(8,128)S(1)}, f32[64,128]{1,0:T(8,128)S(1)}, u32[]{:S(2)}, u32[]{:S(2)}) collective-permute-start(f32[64,128]{1,0:T(8,128)S(1)} %pad_maximum_fusion.even), channel_id=1, source_target_pairs={{0,1},{1,0},{2,3},{3,2},{4,5},{5,4},{6,7},{7,6},{8,9},{9,8},{10,11... | collective-permute-start | bytes 98312 | tf_op jit(solution)/shard_map/ppermute | solution.py:238
  23.9 0.0 collective-permute-done.2.odd
  24.0 2.9 %collective-permute-start.4 = (f32[64,128]{1,0:T(8,128)S(1)}, f32[64,128]{1,0:T(8,128)S(1)}, u32[]{:S(2)}, u32[]{:S(2)}) collective-permute-start(f32[64,128]{1,0:T(8,128)S(1)} %collective-permute-done.2.odd), channel_id=1, source_target_pairs={{0,1},{1,0},{2,3},{3,2},{4,5},{5,4},{6,7},{7,6},{8,9},{9,8},{10,11... | collective-permute-start | bytes 98312 | tf_op jit(solution)/shard_map/ppermute | solution.py:238
  26.8 0.0 collective-permute-done.3.even_c
  26.8 0.9 collective-permute-done.4.odd_c
  27.7 0.3 all-to-all-done.tpg
  28.0 0.0 copy-done
  28.0 3.9 %row_pass_first.1 = (f32[16,1,1152]{2,1,0:T(1,128)S(1)}, bf16[128,1024]{1,0:T(8,128)(2,1)S(1)}, bf16[128,4096]{1,0:T(8,128)(2,1)S(1)}, f32[1,4096]{1,0:T(1,128)S(1)}) custom-call(f32[64,128]{1,0:T(8,128)S(1)} %pad_maximum_fusion.even, f32[64,128]{1,0:T(8,128)S(1)} %collective-permute-done.2.odd, f32[64,128]{1,0:T(8,128)S(1)} %collective-permute-done.3.even_c, ...), custom_call_target="tpu_custom_call" | custom-call | tf_op jit(solution)/shard_map/row_pass_first/pallas_call | solution.py:220
  31.9 13.1 %all_to_all.25.parts = f32[16,1,1152]{2,1,0:T(1,128)S(1)} all-to-all(f32[16,1,1152]{2,1,0:T(1,128)S(1)} %get-tuple-element.16), channel_id=1, replica_groups=mesh['x'=4,'z'=8,'y'=4,'c'=2] {'z','c'}, dimensions={0} | all-to-all | bytes 147456 | tf_op jit(solution)/shard_map/all_to_all | solution.py:233
  45.1 9.0 %column_pass.1 = (f32[16,1,4096]{2,1,0:T(1,128)S(1)}, f32[1,1024]{1,0:T(1,128)S(1)}) custom-call(f32[16,1,1152]{2,1,0:T(1,128)S(1)} %all_to_all.25.parts, bf16[128,1024]{1,0:T(8,128)(2,1)S(1)} %get-tuple-element.17.akm, bf16[128,4096]{1,0:T(8,128)(2,1)S(1)} %get-tuple-element.18.bkm), custom_call_target="tpu_custom_call" | custom-call | tf_op jit(solution)/shard_map/column_pass/pallas_call | solution.py:220
  54.1 11.9 %all_to_all.26.parts = f32[16,1,4096]{2,1,0:T(1,128)S(1)} all-to-all(f32[16,1,4096]{2,1,0:T(1,128)S(1)} %get-tuple-element.19), channel_id=1, replica_groups=mesh['x'=4,'z'=8,'y'=4,'c'=2] {'x','y'}, dimensions={0} | all-to-all | bytes 524288 | tf_op jit(solution)/shard_map/all_to_all | solution.py:233
  66.0 3.1 %row_pass.1 = f32[16,1,1024]{2,1,0:T(1,128)S(1)} custom-call(f32[16,1,4096]{2,1,0:T(1,128)S(1)} %all_to_all.26.parts, f32[1,4096]{1,0:T(1,128)S(1)} %get-tuple-element.20.lb, bf16[128,1024]{1,0:T(8,128)(2,1)S(1)} %get-tuple-element.17.akm, bf16[128,4096]{1,0:T(8,128)(2,1)S(1)} %get-tuple-element.18.bkm), custom_call_target="tpu_custom_call" | custom-call | tf_op jit(solution)/shard_map/row_pass/pallas_call | solution.py:220
  69.1 9.3 %all_to_all.27.parts = f32[16,1,1024]{2,1,0:T(1,128)S(1)} all-to-all(f32[16,1,1024]{2,1,0:T(1,128)S(1)} %row_pass.1), channel_id=1, replica_groups=mesh['x'=4,'z'=8,'y'=4,'c'=2] {'z','c'}, dimensions={0} | all-to-all | bytes 131072 | tf_op jit(solution)/shard_map/all_to_all | solution.py:233
  78.4 9.4 %column_pass_last.1 = (f32[16,1,256]{2,1,0:T(1,128)S(1)}, f32[1,64]{1,0:T(1,128)}) custom-call(f32[16,1,1024]{2,1,0:T(1,128)S(1)} %all_to_all.27.parts, f32[1,1024]{1,0:T(1,128)S(1)} %get-tuple-element.21.la, bf16[128,1024]{1,0:T(8,128)(2,1)S(1)} %get-tuple-element.17.akm, bf16[128,4096]{1,0:T(8,128)(2,1)S(1)} %get-tuple-element.18.bkm, ...), custom_call_target="tpu_custom_call" | custom-call | tf_op jit(solution)/shard_map/column_pass_last/pallas_call | solution.py:220
  87.8 9.6 %all_to_all.28.parts = f32[16,1,256]{2,1,0:T(1,128)S(1)} all-to-all(f32[16,1,256]{2,1,0:T(1,128)S(1)} %get-tuple-element.24), channel_id=1, replica_groups=mesh['x'=4,'z'=8,'y'=4,'c'=2] {'x','y'}, dimensions={0} | all-to-all | bytes 32768 | tf_op jit(solution)/shard_map/all_to_all | solution.py:233
  97.4 0.6 last.1
  (2 shorter events, 0.0 us)
Async XLA Ops:
  2.3 14.6 %collective-permute-start = (f32[16,128]{1,0:T(8,128)S(1)}, f32[16,128]{1,0:T(8,128)S(1)}, u32[]{:S(2)}, u32[]{:S(2)}) collective-permute-start(f32[16,128]{1,0:T(8,128)S(1)} %get-tuple-element.14.first), channel_id=1, source_target_pairs={{0,32},{8,40},{16,48},{24,56},{32,0},{40,8},{48,16},{56,24},{1,33}... | collective-permute-start | bytes 24584 | tf_op jit(solution)/shard_map/ppermute | solution.py:238
  10.1 17.9 %all-to-all-start = ((f32[16,72,128]{2,1,0:T(8,128)}), f32[16,72,128]{2,1,0:T(8,128)}, u32[]{:S(2)}, u32[]{:S(2)}) async-start(f32[16,72,128]{2,1,0:T(8,128)} %get-tuple-element.15), calls=%async_computation | async-start | bytes 1179648 | tf_op jit(solution)/shard_map/all_to_all | solution.py:233
  17.0 3.6 %collective-permute-start.1 = (f32[32,128]{1,0:T(8,128)S(1)}, f32[32,128]{1,0:T(8,128)S(1)}, u32[]{:S(2)}, u32[]{:S(2)}) collective-permute-start(f32[32,128]{1,0:T(8,128)S(1)} %join.1), channel_id=1, source_target_pairs={{0,16},{8,24},{16,0},{24,8},{32,48},{40,56},{48,32},{56,40},{1,17}... | collective-permute-start | bytes 49160 | tf_op jit(solution)/shard_map/ppermute | solution.py:238
  20.5 7.4 %copy-start = (f32[64]{0:T(128)S(1)}, f32[64]{0:T(128)}, u32[]{:S(2)}) copy-start(f32[64]{0:T(128)} %param.6) | copy-start | bytes 772
  20.5 3.4 %collective-permute-start.2 = (f32[64,128]{1,0:T(8,128)S(1)}, f32[64,128]{1,0:T(8,128)S(1)}, u32[]{:S(2)}, u32[]{:S(2)}) collective-permute-start(f32[64,128]{1,0:T(8,128)S(1)} %pad_maximum_fusion.even), channel_id=1, source_target_pairs={{0,8},{8,0},{16,24},{24,16},{32,40},{40,32},{48,56},{56,48},{1,9},... | collective-permute-start | bytes 98312 | tf_op jit(solution)/shard_map/ppermute | solution.py:238
  21.3 5.6 %collective-permute-start.3 = (f32[64,128]{1,0:T(8,128)S(1)}, f32[64,128]{1,0:T(8,128)S(1)}, u32[]{:S(2)}, u32[]{:S(2)}) collective-permute-start(f32[64,128]{1,0:T(8,128)S(1)} %pad_maximum_fusion.even), channel_id=1, source_target_pairs={{0,1},{1,0},{2,3},{3,2},{4,5},{5,4},{6,7},{7,6},{8,9},{9,8},{10,11... | collective-permute-start | bytes 98312 | tf_op jit(solution)/shard_map/ppermute | solution.py:238
  24.0 3.8 %collective-permute-start.4 = (f32[64,128]{1,0:T(8,128)S(1)}, f32[64,128]{1,0:T(8,128)S(1)}, u32[]{:S(2)}, u32[]{:S(2)}) collective-permute-start(f32[64,128]{1,0:T(8,128)S(1)} %collective-permute-done.2.odd), channel_id=1, source_target_pairs={{0,1},{1,0},{2,3},{3,2},{4,5},{5,4},{6,7},{7,6},{8,9},{9,8},{10,11... | collective-permute-start | bytes 98312 | tf_op jit(solution)/shard_map/ppermute | solution.py:238
